TPU v7x, 32 devices: a whole 2x2x4 slice. The times are simulated.
32 devices in a mesh: section: 2 (over x), tensor: 4 (over z), dp: 4 (over y, core).
Axes of the slice: x: 2, y: 2, z: 4, core: 2. Of those that a mesh axis runs over, the one named last changes fastest.
Arguments:
- frames: bfloat16 [8, 128, 768], P('dp'), may hold values from -6 to 6
- cotangent: bfloat16 [8, 128, 768], P('dp'), may hold values from -6 to 6
- gain_one: float32 [2, 768], P('section'), may hold values from 0.25 to 1.75
- shift_one: float32 [2, 768], P('section'), may hold values from -1.5 to 1.5
- w_query: bfloat16 [2, 768, 768], P('section', None, 'tensor'), may hold values from -0.21875 to 0.21875
- query_bias: float32 [2, 768], P('section', 'tensor'), may hold values from -1.5 to 1.5
- w_key: bfloat16 [2, 768, 768], P('section', None, 'tensor'), may hold values from -0.21875 to 0.21875
- w_value: bfloat16 [2, 768, 768], P('section', None, 'tensor'), may hold values from -0.21875 to 0.21875
- value_bias: float32 [2, 768], P('section', 'tensor'), may hold values from -1.5 to 1.5
- w_attn: bfloat16 [2, 768, 768], P('section', 'tensor'), may hold values from -0.875 to 0.875
- attn_bias: float32 [2, 768], P('section'), may hold values from -1.5 to 1.5
- gain_two: float32 [2, 768], P('section'), may hold values from 0.25 to 1.75
- shift_two: float32 [2, 768], P('section'), may hold values from -1.5 to 1.5
- w_inner: bfloat16 [2, 768, 3072], P('section', None, 'tensor'), may hold values from -0.21875 to 0.21875
- inner_bias: float32 [2, 3072], P('section', 'tensor'), may hold values from -1.5 to 1.5
- w_outer: bfloat16 [2, 3072, 768], P('section', 'tensor'), may hold values from -0.109375 to 0.109375
- outer_bias: float32 [2, 768], P('section'), may hold values from -1.5 to 1.5
Outputs:
- layer_outputs: bfloat16 [2, 8, 128, 768], P('section', 'dp')
- layer_input_grads: bfloat16 [2, 8, 128, 768], P('section', 'dp')
- grad_gain_one: float32 [2, 768], P('section', 'dp')
- grad_shift_one: float32 [2, 768], P('section', 'dp')
- grad_w_query: float32 [2, 768, 768], P('section', 'dp', 'tensor')
- grad_query_bias: float32 [2, 768], P('section', ('tensor', 'dp'))
- grad_w_key: float32 [2, 768, 768], P('section', 'dp', 'tensor')
- grad_w_value: float32 [2, 768, 768], P('section', 'dp', 'tensor')
- grad_value_bias: float32 [2, 768], P('section', ('tensor', 'dp'))
- grad_w_attn: float32 [2, 768, 768], P('section', ('tensor', 'dp'))
- grad_attn_bias: float32 [2, 768], P('section', 'dp')
- grad_gain_two: float32 [2, 768], P('section', 'dp')
- grad_shift_two: float32 [2, 768], P('section', 'dp')
- grad_w_inner: float32 [2, 768, 3072], P('section', 'dp', 'tensor')
- grad_inner_bias: float32 [2, 3072], P('section', ('tensor', 'dp'))
- grad_w_outer: float32 [2, 3072, 768], P('section', ('tensor', 'dp'))
- grad_outer_bias: float32 [2, 768], P('section', 'dp')
All inputs are finite; a program needn't handle non-finite values.
Results may differ from a plain program's by a relative error of at most 0.025.
Values may be sent and summed in bfloat16 or wider, within the bound.
A program may use at most 128 MiB of HBM per device.

v0:
```python
from functools import partial

import jax
import jax.numpy as jnp
from jax import lax
from jax.sharding import PartitionSpec as P

HEAD_DIM = 64


epsilon = 1e-05


def shifted(block, axis, distance):
    devices = range(lax.axis_size(axis))
    route = [(i - distance, i) for i in devices if i - distance in devices]
    return lax.ppermute(block, axis, route)


def normalize(values, gain, shift):
    center = values - jnp.mean(values, axis=-1, keepdims=True)
    spread = jnp.mean(center * center, axis=-1, keepdims=True)
    return center * lax.rsqrt(spread + epsilon) * gain + shift


def split_heads(values):
    return values.reshape(values.shape[0], -1, HEAD_DIM)


def gelu_exact(values):
    return jax.nn.gelu(values, approximate=False)


def layer_forward(inputs, weights):
    (
        gain_one,
        shift_one,
        w_query,
        query_bias,
        w_key,
        w_value,
        value_bias,
        w_attn,
        attn_bias,
        gain_two,
        shift_two,
        w_inner,
        inner_bias,
        w_outer,
        outer_bias,
    ) = weights
    values = inputs.astype(jnp.float32)
    normed = normalize(values, gain_one, shift_one).astype(jnp.bfloat16)
    queries = (jnp.dot(normed, w_query, preferred_element_type=jnp.float32) + query_bias).astype(
        jnp.bfloat16
    )
    key_rows = jnp.dot(normed, w_key, preferred_element_type=jnp.float32).astype(jnp.bfloat16)
    value_rows = (jnp.dot(normed, w_value, preferred_element_type=jnp.float32) + value_bias).astype(
        jnp.bfloat16
    )
    scores = jnp.einsum(
        "shd,thd->hst",
        split_heads(queries),
        split_heads(key_rows),
        preferred_element_type=jnp.float32,
    ) * HEAD_DIM ** (-0.5)
    row_peak = jnp.max(scores, axis=-1, keepdims=True)
    row_total = jnp.log(jnp.sum(jnp.exp(scores - row_peak), axis=-1, keepdims=True)) + row_peak
    probs = jnp.exp(scores - row_total).astype(jnp.bfloat16)
    mixed = jnp.einsum(
        "hst,thd->shd", probs, split_heads(value_rows), preferred_element_type=jnp.float32
    )
    mixed = mixed.reshape(values.shape[0], -1).astype(jnp.bfloat16)
    attention = lax.psum(
        jnp.dot(mixed, w_attn, preferred_element_type=jnp.float32).astype(jnp.bfloat16), "tensor"
    ).astype(jnp.float32)
    middle = values + attention + attn_bias
    normed_two = normalize(middle, gain_two, shift_two).astype(jnp.bfloat16)
    hidden_pre = jnp.dot(normed_two, w_inner, preferred_element_type=jnp.float32) + inner_bias
    active = gelu_exact(hidden_pre).astype(jnp.bfloat16)
    feed = lax.psum(
        jnp.dot(active, w_outer, preferred_element_type=jnp.float32).astype(jnp.bfloat16), "tensor"
    ).astype(jnp.float32)
    result = middle + feed + outer_bias
    kept = (inputs, middle, queries, key_rows, value_rows, mixed, row_total, hidden_pre)
    return (result, kept)


def feed_forward_back(grad_out, kept, weights):
    (
        gain_one,
        shift_one,
        w_query,
        query_bias,
        w_key,
        w_value,
        value_bias,
        w_attn,
        attn_bias,
        gain_two,
        shift_two,
        w_inner,
        inner_bias,
        w_outer,
        outer_bias,
    ) = weights
    inputs, middle, queries, key_rows, value_rows, mixed, row_total, hidden_pre = kept
    grad_low = grad_out.astype(jnp.bfloat16)
    outer_bias_grad = jnp.sum(grad_out, axis=0)
    active, gelu_back = jax.vjp(gelu_exact, hidden_pre)
    active_low = active.astype(jnp.bfloat16)
    active_grad = jnp.einsum("sd,fd->sf", grad_low, w_outer, preferred_element_type=jnp.float32)
    (hidden_grad,) = gelu_back(active_grad)
    inner_bias_grad = jnp.sum(hidden_grad, axis=0)
    hidden_low = hidden_grad.astype(jnp.bfloat16)
    normed_two, norm_back = jax.vjp(normalize, middle, gain_two, shift_two)
    normed_low = normed_two.astype(jnp.bfloat16)
    normed_grad = lax.psum(
        jnp.einsum("sf,df->sd", hidden_low, w_inner, preferred_element_type=jnp.float32).astype(
            jnp.bfloat16
        ),
        "tensor",
    ).astype(jnp.float32)
    middle_grad, gain_two_grad, shift_two_grad = norm_back(normed_grad)
    middle_grad = middle_grad + grad_out
    smalls = (gain_two_grad, shift_two_grad, inner_bias_grad, outer_bias_grad)
    operands = (normed_low, hidden_low, active_low, grad_low)
    return (middle_grad, smalls, operands)


def feed_weights(smalls, operand_list):
    normed_all, hidden_all, active_all, grad_all = [
        jnp.concatenate([ops[index] for ops in operand_list], axis=0) for index in range(4)
    ]
    w_inner_grad = jnp.einsum(
        "sd,sf->df", normed_all, hidden_all, preferred_element_type=jnp.float32
    )
    w_outer_grad = jnp.einsum("sf,sd->fd", active_all, grad_all, preferred_element_type=jnp.float32)
    return (smalls[0], smalls[1], w_inner_grad, smalls[2], w_outer_grad, smalls[3])


def attention_back(grad_mid, kept, weights):
    (
        gain_one,
        shift_one,
        w_query,
        query_bias,
        w_key,
        w_value,
        value_bias,
        w_attn,
        attn_bias,
        gain_two,
        shift_two,
        w_inner,
        inner_bias,
        w_outer,
        outer_bias,
    ) = weights
    inputs, middle, queries, key_rows, value_rows, mixed, row_total, hidden_pre = kept
    scale = HEAD_DIM ** (-0.5)
    grad_low = grad_mid.astype(jnp.bfloat16)
    attn_bias_grad = jnp.sum(grad_mid, axis=0)
    mixed_grad = jnp.einsum(
        "sd,cd->sc", grad_low, w_attn, preferred_element_type=jnp.float32
    ).astype(jnp.bfloat16)
    query_heads = split_heads(queries)
    key_heads = split_heads(key_rows)
    value_heads = split_heads(value_rows)
    mixed_heads = split_heads(mixed_grad)
    scores = (
        jnp.einsum("shd,thd->hst", query_heads, key_heads, preferred_element_type=jnp.float32)
        * scale
    )
    probs = jnp.exp(scores - row_total)
    value_grad = jnp.einsum(
        "hst,shd->thd", probs.astype(jnp.bfloat16), mixed_heads, preferred_element_type=jnp.float32
    )
    prob_grad = jnp.einsum(
        "shd,thd->hst", mixed_heads, value_heads, preferred_element_type=jnp.float32
    )
    score_grad = (probs * (prob_grad - jnp.sum(prob_grad * probs, axis=-1, keepdims=True))).astype(
        jnp.bfloat16
    )
    query_grad = (
        jnp.einsum("hst,thd->shd", score_grad, key_heads, preferred_element_type=jnp.float32)
        * scale
    )
    key_grad = (
        jnp.einsum("hst,shd->thd", score_grad, query_heads, preferred_element_type=jnp.float32)
        * scale
    )
    rows_count = queries.shape[0]
    query_grad = query_grad.reshape(rows_count, -1)
    key_grad = key_grad.reshape(rows_count, -1)
    value_grad = value_grad.reshape(rows_count, -1)
    query_bias_grad = jnp.sum(query_grad, axis=0)
    value_bias_grad = jnp.sum(value_grad, axis=0)
    query_low = query_grad.astype(jnp.bfloat16)
    key_low = key_grad.astype(jnp.bfloat16)
    value_low = value_grad.astype(jnp.bfloat16)
    normed, norm_back = jax.vjp(normalize, inputs.astype(jnp.float32), gain_one, shift_one)
    normed_low = normed.astype(jnp.bfloat16)
    partial_grad = jnp.einsum("sc,dc->sd", query_low, w_query, preferred_element_type=jnp.float32)
    partial_grad = partial_grad + jnp.einsum(
        "sc,dc->sd", key_low, w_key, preferred_element_type=jnp.float32
    )
    partial_grad = partial_grad + jnp.einsum(
        "sc,dc->sd", value_low, w_value, preferred_element_type=jnp.float32
    )
    normed_grad = lax.psum(partial_grad.astype(jnp.bfloat16), "tensor").astype(jnp.float32)
    input_grad, gain_one_grad, shift_one_grad = norm_back(normed_grad)
    input_grad = input_grad + grad_mid
    smalls = (gain_one_grad, shift_one_grad, query_bias_grad, value_bias_grad, attn_bias_grad)
    operands = (mixed, grad_low, normed_low, query_low, key_low, value_low)
    return (input_grad, smalls, operands)


def attention_weights(smalls, operand_list):
    mixed_all, grad_all, normed_all, query_all, key_all, value_all = [
        jnp.concatenate([ops[index] for ops in operand_list], axis=0) for index in range(6)
    ]
    w_attn_grad = jnp.einsum("sc,sd->cd", mixed_all, grad_all, preferred_element_type=jnp.float32)
    w_query_grad = jnp.einsum(
        "sd,sc->dc", normed_all, query_all, preferred_element_type=jnp.float32
    )
    w_key_grad = jnp.einsum("sd,sc->dc", normed_all, key_all, preferred_element_type=jnp.float32)
    w_value_grad = jnp.einsum(
        "sd,sc->dc", normed_all, value_all, preferred_element_type=jnp.float32
    )
    return (
        smalls[0],
        smalls[1],
        w_query_grad,
        smalls[2],
        w_key_grad,
        w_value_grad,
        smalls[3],
        w_attn_grad,
        smalls[4],
    )


def local(
    frames,
    cotangent,
    gain_one,
    shift_one,
    w_query,
    query_bias,
    w_key,
    w_value,
    value_bias,
    w_attn,
    attn_bias,
    gain_two,
    shift_two,
    w_inner,
    inner_bias,
    w_outer,
    outer_bias,
):
    weights = tuple(
        (
            stacked[0]
            for stacked in (
                gain_one,
                shift_one,
                w_query,
                query_bias,
                w_key,
                w_value,
                value_bias,
                w_attn,
                attn_bias,
                gain_two,
                shift_two,
                w_inner,
                inner_bias,
                w_outer,
                outer_bias,
            )
        )
    )
    first_section = lax.axis_index("section") == 0
    clip_count = frames.shape[0]
    plane = frames.shape[1:]

    def choose(early_value, late_value):
        return jax.tree.map(partial(jnp.where, first_section), early_value, late_value)

    handed = jnp.zeros(plane, jnp.bfloat16)
    results = []
    saved = []
    for moment in range(clip_count + 1):
        if moment > 0:
            arrived = shifted(handed, "section", 1)
        else:
            arrived = jnp.zeros(plane, jnp.bfloat16)
        entering = jnp.where(first_section, frames[min(moment, clip_count - 1)], arrived)
        result, kept = layer_forward(entering, weights)
        handed = result.astype(jnp.bfloat16)
        results.append(handed)
        saved.append(kept)
    layer_outputs = jnp.stack(
        [choose(results[index], results[index + 1]) for index in range(clip_count)]
    )
    kept_clips = [choose(saved[index], saved[index + 1]) for index in range(clip_count)]
    returned = jnp.zeros(plane, jnp.bfloat16)
    attention_small = None
    feed_small = None
    attention_ops = []
    feed_ops = []
    sent_grads = []
    for moment in range(clip_count + 1):
        if moment > 0:
            arrived = shifted(returned, "section", -1).astype(jnp.float32)
        else:
            arrived = jnp.zeros(plane, jnp.float32)
        if moment < clip_count:
            upstream = cotangent[moment].astype(jnp.float32)
        else:
            upstream = jnp.zeros(plane, jnp.float32)
        grad_out = jnp.where(first_section, arrived, upstream)
        kept = choose(kept_clips[max(moment - 1, 0)], kept_clips[min(moment, clip_count - 1)])
        middle_grad, feed_part, feed_operands = feed_forward_back(grad_out, kept, weights)
        feed_ops.append(feed_operands)
        if feed_small is None:
            feed_small = feed_part
        else:
            feed_small = jax.tree.map(jnp.add, feed_small, feed_part)
        if moment == clip_count:
            feed_total = feed_weights(feed_small, feed_ops)
        input_grad, attention_part, attention_operands = attention_back(middle_grad, kept, weights)
        attention_ops.append(attention_operands)
        if attention_small is None:
            attention_small = attention_part
        else:
            attention_small = jax.tree.map(jnp.add, attention_small, attention_part)
        returned = input_grad.astype(jnp.bfloat16)
        sent_grads.append(returned)
    layer_input_grads = jnp.stack(
        [choose(sent_grads[index + 1], sent_grads[index]) for index in range(clip_count)]
    )
    attention_total = attention_weights(attention_small, attention_ops)
    every_part = [member[None] for member in tuple(attention_total) + tuple(feed_total)]
    reduced = (
        lax.psum_scatter(
            every_part[0].astype(jnp.bfloat16), "dp", scatter_dimension=1, tiled=True
        ).astype(jnp.float32),
        lax.psum_scatter(
            every_part[1].astype(jnp.bfloat16), "dp", scatter_dimension=1, tiled=True
        ).astype(jnp.float32),
        lax.psum_scatter(
            every_part[2].astype(jnp.bfloat16), "dp", scatter_dimension=1, tiled=True
        ).astype(jnp.float32),
        lax.psum_scatter(
            every_part[3].astype(jnp.bfloat16), "dp", scatter_dimension=1, tiled=True
        ).astype(jnp.float32),
        lax.psum_scatter(
            every_part[4].astype(jnp.bfloat16), "dp", scatter_dimension=1, tiled=True
        ).astype(jnp.float32),
        lax.psum_scatter(
            every_part[5].astype(jnp.bfloat16), "dp", scatter_dimension=1, tiled=True
        ).astype(jnp.float32),
        lax.psum_scatter(
            every_part[6].astype(jnp.bfloat16), "dp", scatter_dimension=1, tiled=True
        ).astype(jnp.float32),
        lax.psum_scatter(
            every_part[7].astype(jnp.bfloat16), "dp", scatter_dimension=1, tiled=True
        ).astype(jnp.float32),
        lax.psum_scatter(
            every_part[8].astype(jnp.bfloat16), "dp", scatter_dimension=1, tiled=True
        ).astype(jnp.float32),
        lax.psum_scatter(
            every_part[9].astype(jnp.bfloat16), "dp", scatter_dimension=1, tiled=True
        ).astype(jnp.float32),
        lax.psum_scatter(
            every_part[10].astype(jnp.bfloat16), "dp", scatter_dimension=1, tiled=True
        ).astype(jnp.float32),
        lax.psum_scatter(
            every_part[11].astype(jnp.bfloat16), "dp", scatter_dimension=1, tiled=True
        ).astype(jnp.float32),
        lax.psum_scatter(
            every_part[12].astype(jnp.bfloat16), "dp", scatter_dimension=1, tiled=True
        ).astype(jnp.float32),
        lax.psum_scatter(
            every_part[13].astype(jnp.bfloat16), "dp", scatter_dimension=1, tiled=True
        ).astype(jnp.float32),
        lax.psum_scatter(
            every_part[14].astype(jnp.bfloat16), "dp", scatter_dimension=1, tiled=True
        ).astype(jnp.float32),
    )
    return (
        layer_outputs[None],
        layer_input_grads[None],
        reduced[0],
        reduced[1],
        reduced[2],
        reduced[3],
        reduced[4],
        reduced[5],
        reduced[6],
        reduced[7],
        reduced[8],
        reduced[9],
        reduced[10],
        reduced[11],
        reduced[12],
        reduced[13],
        reduced[14],
    )


def solution(mesh):
    in_specs = (
        P("dp", None, None),
        P("dp", None, None),
        P("section", None),
        P("section", None),
        P("section", None, "tensor"),
        P("section", "tensor"),
        P("section", None, "tensor"),
        P("section", None, "tensor"),
        P("section", "tensor"),
        P("section", "tensor", None),
        P("section", None),
        P("section", None),
        P("section", None),
        P("section", None, "tensor"),
        P("section", "tensor"),
        P("section", "tensor", None),
        P("section", None),
    )
    out_specs = (
        P("section", "dp", None, None),
        P("section", "dp", None, None),
        P("section", "dp"),
        P("section", "dp"),
        P("section", "dp", "tensor"),
        P("section", ("tensor", "dp")),
        P("section", "dp", "tensor"),
        P("section", "dp", "tensor"),
        P("section", ("tensor", "dp")),
        P("section", ("tensor", "dp"), None),
        P("section", "dp"),
        P("section", "dp"),
        P("section", "dp"),
        P("section", "dp", "tensor"),
        P("section", ("tensor", "dp")),
        P("section", ("tensor", "dp"), None),
        P("section", "dp"),
    )
    return jax.shard_map(local, mesh=mesh, in_specs=in_specs, out_specs=out_specs, check_vma=False)
```

profile of v0, /device:TPU:0, one launch (start us, length us, event | category | flops | bytes accessed | tf_op | source)
XLA Modules:
  0.0 799.1 jit_solution(4749203131698793721)
XLA Ops:
  15.0 37.5 %all-reduce.13.cloned.1.call-done = bf16[128,768]{1,0:T(8,128)(2,1)} async-done(((bf16[128,768]{1,0:T(8,128)(2,1)}), bf16[128,768]{1,0:T(8,128)(2,1)}) %all-reduce.13.cloned.1.call-update) | async-done | bytes 196624 | tf_op jit(solution)/shard_map/psum | solution.py:74
  58.1 34.6 %all-reduce.15.cloned.1.call-done = bf16[128,768]{1,0:T(8,128)(2,1)} async-done(((bf16[128,768]{1,0:T(8,128)(2,1)}), bf16[128,768]{1,0:T(8,128)(2,1)}) %all-reduce.15.cloned.1.call-update) | async-done | bytes 196624 | tf_op jit(solution)/shard_map/psum | solution.py:81
  103.7 35.6 %all-reduce.17.cloned.1.call-done = bf16[128,768]{1,0:T(8,128)(2,1)} async-done(((bf16[128,768]{1,0:T(8,128)(2,1)}), bf16[128,768]{1,0:T(8,128)(2,1)}) %all-reduce.17.cloned.1.call-update) | async-done | bytes 196624 | tf_op jit(solution)/shard_map/psum | solution.py:74
  148.6 36.9 %all-reduce.29.cloned.1.call-done = (bf16[128,768]{1,0:T(8,128)(2,1)}, bf16[128,768]{1,0:T(8,128)(2,1)}) async-done(((bf16[128,768]{1,0:T(8,128)(2,1)}, bf16[128,768]{1,0:T(8,128)(2,1)}), (bf16[128,768]{1,0:T(8,128)(2,1)}, bf16[128,768]{1,0:T(8,128)(2,1)})) %all-reduce.29.cloned.1.call-update) | async-done | bytes 393232 | tf_op jit(solution)/shard_map/psum | solution.py:81
  214.2 33.3 %all-reduce.27.cloned.1.call-done = (bf16[128,768]{1,0:T(8,128)(2,1)}, bf16[128,768]{1,0:T(8,128)(2,1)}) async-done(((bf16[128,768]{1,0:T(8,128)(2,1)}, bf16[128,768]{1,0:T(8,128)(2,1)}), (bf16[128,768]{1,0:T(8,128)(2,1)}, bf16[128,768]{1,0:T(8,128)(2,1)})) %all-reduce.27.cloned.1.call-update) | async-done | bytes 393232 | tf_op jit(solution)/shard_map/psum | solution.py:211
  264.4 35.1 %all-reduce.19.cloned.1.call-done = bf16[128,768]{1,0:T(8,128)(2,1)} async-done(((bf16[128,768]{1,0:T(8,128)(2,1)}), bf16[128,768]{1,0:T(8,128)(2,1)}) %all-reduce.19.cloned.1.call-update) | async-done | bytes 196624 | tf_op jit(solution)/shard_map/psum | solution.py:118
  310.1 34.6 %all-reduce.21.cloned.1.call-done = bf16[128,768]{1,0:T(8,128)(2,1)} async-done(((bf16[128,768]{1,0:T(8,128)(2,1)}), bf16[128,768]{1,0:T(8,128)(2,1)}) %all-reduce.21.cloned.1.call-update) | async-done | bytes 196624 | tf_op jit(solution)/shard_map/psum | solution.py:211
  353.5 4.2 collective-permute-done.3
  361.0 33.7 %all-reduce.23.cloned.1.call-done = bf16[128,768]{1,0:T(8,128)(2,1)} async-done(((bf16[128,768]{1,0:T(8,128)(2,1)}), bf16[128,768]{1,0:T(8,128)(2,1)}) %all-reduce.23.cloned.1.call-update) | async-done | bytes 196624 | tf_op jit(solution)/shard_map/psum | solution.py:118
  410.9 30.2 %all-reduce.25.cloned.1.call-done = (bf16[128,768]{1,0:T(8,128)(2,1)}, bf16[128,768]{1,0:T(8,128)(2,1)}) async-done(((bf16[128,768]{1,0:T(8,128)(2,1)}, bf16[128,768]{1,0:T(8,128)(2,1)}), (bf16[128,768]{1,0:T(8,128)(2,1)}, bf16[128,768]{1,0:T(8,128)(2,1)})) %all-reduce.25.cloned.1.call-update) | async-done | bytes 393232 | tf_op jit(solution)/shard_map/psum | solution.py:211
  464.7 20.0 %reduce-scatter.52.cloned.1.call-done = bf16[48,1]{1,0:T(8,128)(2,1)} async-done(((bf16[192,1]{1,0:T(8,128)(2,1)}), bf16[48,1]{1,0:T(8,128)(2,1)}) %reduce-scatter.52.cloned.1.call-update) | async-done | bytes 112
  486.1 20.4 %reduce-scatter.58.cloned.1.call-done = bf16[48,1]{1,0:T(8,128)(2,1)} async-done(((bf16[192,1]{1,0:T(8,128)(2,1)}), bf16[48,1]{1,0:T(8,128)(2,1)}) %reduce-scatter.58.cloned.1.call-update) | async-done | bytes 112
  507.8 21.0 %reduce-scatter.60.cloned.1.call-done = bf16[192,1]{1,0:T(8,128)(2,1)} async-done(((bf16[768,1]{1,0:T(8,128)(2,1)}), bf16[192,1]{1,0:T(8,128)(2,1)}) %reduce-scatter.60.cloned.1.call-update) | async-done | bytes 400
  530.3 20.7 %reduce-scatter.62.cloned.1.call-done = bf16[192,1]{1,0:T(8,128)(2,1)} async-done(((bf16[768,1]{1,0:T(8,128)(2,1)}), bf16[192,1]{1,0:T(8,128)(2,1)}) %reduce-scatter.62.cloned.1.call-update) | async-done | bytes 400
  552.5 20.7 %reduce-scatter.64.cloned.1.call-done = bf16[192,1]{1,0:T(8,128)(2,1)} async-done(((bf16[768,1]{1,0:T(8,128)(2,1)}), bf16[192,1]{1,0:T(8,128)(2,1)}) %reduce-scatter.64.cloned.1.call-update) | async-done | bytes 400
  574.7 20.7 %reduce-scatter.68.cloned.1.call-done = bf16[192,1]{1,0:T(8,128)(2,1)} async-done(((bf16[768,1]{1,0:T(8,128)(2,1)}), bf16[192,1]{1,0:T(8,128)(2,1)}) %reduce-scatter.68.cloned.1.call-update) | async-done | bytes 400
  599.9 17.7 %reduce-scatter.46.cloned.1.call-done = bf16[192,1]{1,0:T(8,128)(2,1)} async-done(((bf16[768,1]{1,0:T(8,128)(2,1)}), bf16[192,1]{1,0:T(8,128)(2,1)}) %reduce-scatter.46.cloned.1.call-update) | async-done | bytes 400
  619.1 20.7 %reduce-scatter.48.cloned.1.call-done = bf16[192,1]{1,0:T(8,128)(2,1)} async-done(((bf16[768,1]{1,0:T(8,128)(2,1)}), bf16[192,1]{1,0:T(8,128)(2,1)}) %reduce-scatter.48.cloned.1.call-update) | async-done | bytes 400
  641.3 21.4 %reduce-scatter.40.cloned.1.call-done = bf16[1,48,768]{2,1,0:T(8,128)(2,1)} async-done(((bf16[1,192,768]{2,1,0:T(8,128)(2,1)}), bf16[1,48,768]{2,1,0:T(8,128)(2,1)}) %reduce-scatter.40.cloned.1.call-update) | async-done | bytes 73744 | tf_op jit(solution)/shard_map/reduce_scatter | solution.py:369
  664.3 22.2 %reduce-scatter.50.cloned.1.call-done = bf16[192,192]{1,0:T(8,128)(2,1)} async-done(((bf16[768,192]{1,0:T(8,128)(2,1)}), bf16[192,192]{1,0:T(8,128)(2,1)}) %reduce-scatter.50.cloned.1.call-update) | async-done | bytes 73744
  688.4 22.0 %reduce-scatter.54.cloned.1.call-done = bf16[192,192]{1,0:T(8,128)(2,1)} async-done(((bf16[768,192]{1,0:T(8,128)(2,1)}), bf16[192,192]{1,0:T(8,128)(2,1)}) %reduce-scatter.54.cloned.1.call-update) | async-done | bytes 73744
  712.4 21.4 %reduce-scatter.56.cloned.1.call-done = bf16[192,192]{1,0:T(8,128)(2,1)} async-done(((bf16[768,192]{1,0:T(8,128)(2,1)}), bf16[192,192]{1,0:T(8,128)(2,1)}) %reduce-scatter.56.cloned.1.call-update) | async-done | bytes 73744
  735.7 26.4 %reduce-scatter.44.cloned.1.call-done = bf16[1,192,768]{2,1,0:T(8,128)(2,1)} async-done(((bf16[1,768,768]{2,1,0:T(8,128)(2,1)}), bf16[1,192,768]{2,1,0:T(8,128)(2,1)}) %reduce-scatter.44.cloned.1.call-update) | async-done | bytes 294928 | tf_op jit(solution)/shard_map/reduce_scatter | solution.py:387
  763.9 26.5 %reduce-scatter.42.cloned.1.call-done = bf16[1,192,768]{2,1,0:T(8,128)(2,1)} async-done(((bf16[1,768,768]{2,1,0:T(8,128)(2,1)}), bf16[1,192,768]{2,1,0:T(8,128)(2,1)}) %reduce-scatter.42.cloned.1.call-update) | async-done | bytes 294928 | tf_op jit(solution)/shard_map/reduce_scatter | solution.py:381
  (606 shorter events, 164.4 us)
Async XLA Ops:
  7.2 45.2 %all-reduce.13.cloned.1.call-start = ((), (), s32[]{:S(2)}) async-start(), calls=%async_computation.15 | async-start | bytes 393216 | tf_op jit(solution)/shard_map/psum | solution.py:74
  14.8 77.9 %all-reduce.15.cloned.1.call-start = ((), (), s32[]{:S(2)}) async-start(), calls=%async_computation.16 | async-start | bytes 393216 | tf_op jit(solution)/shard_map/psum | solution.py:81
  58.0 81.4 %all-reduce.17.cloned.1.call-start = ((), (), s32[]{:S(2)}) async-start(), calls=%async_computation.17 | async-start | bytes 393216 | tf_op jit(solution)/shard_map/psum | solution.py:74
  103.7 81.8 %all-reduce.29.cloned.1.call-start = ((), (), s32[]{:S(2)}) async-start(), calls=%async_computation.38 | async-start | bytes 786432 | tf_op jit(solution)/shard_map/psum | solution.py:81
  148.6 98.9 %all-reduce.27.cloned.1.call-start = ((), (), s32[]{:S(2)}) async-start(), calls=%async_computation.37 | async-start | bytes 786432 | tf_op jit(solution)/shard_map/psum | solution.py:211
  209.7 89.8 %all-reduce.19.cloned.1.call-start = ((), (), s32[]{:S(2)}) async-start(), calls=%async_computation.18 | async-start | bytes 393216 | tf_op jit(solution)/shard_map/psum | solution.py:118
  264.3 80.4 %all-reduce.21.cloned.1.call-start = ((), (), s32[]{:S(2)}) async-start(), calls=%async_computation.19 | async-start | bytes 393216 | tf_op jit(solution)/shard_map/psum | solution.py:211
  310.0 84.7 %all-reduce.23.cloned.1.call-start = ((), (), s32[]{:S(2)}) async-start(), calls=%async_computation.20 | async-start | bytes 393216 | tf_op jit(solution)/shard_map/psum | solution.py:118
  360.9 80.2 %all-reduce.25.cloned.1.call-start = ((), (), s32[]{:S(2)}) async-start(), calls=%async_computation.36 | async-start | bytes 786432 | tf_op jit(solution)/shard_map/psum | solution.py:211
  404.2 58.9 %reduce-scatter.66.cloned.1.call-start = ((), (), s32[]{:S(2)}) async-start(), calls=%async_computation.34 | async-start | bytes 245760
  405.2 79.6 %reduce-scatter.52.cloned.1.call-start = ((), (), s32[]{:S(2)}) async-start(), calls=%async_computation.27 | async-start | bytes 61440
  406.0 100.4 %reduce-scatter.58.cloned.1.call-start = ((), (), s32[]{:S(2)}) async-start(), calls=%async_computation.30 | async-start | bytes 61440
  406.9 121.9 %reduce-scatter.60.cloned.1.call-start = ((), (), s32[]{:S(2)}) async-start(), calls=%async_computation.31 | async-start | bytes 245760
  407.9 143.1 %reduce-scatter.62.cloned.1.call-start = ((), (), s32[]{:S(2)}) async-start(), calls=%async_computation.32 | async-start | bytes 245760
  408.9 164.3 %reduce-scatter.64.cloned.1.call-start = ((), (), s32[]{:S(2)}) async-start(), calls=%async_computation.33 | async-start | bytes 245760
  409.9 185.5 %reduce-scatter.68.cloned.1.call-start = ((), (), s32[]{:S(2)}) async-start(), calls=%async_computation.35 | async-start | bytes 245760
  410.9 206.7 %reduce-scatter.46.cloned.1.call-start = ((), (), s32[]{:S(2)}) async-start(), calls=%async_computation.24 | async-start | bytes 245760
  445.6 194.2 %reduce-scatter.48.cloned.1.call-start = ((), (), s32[]{:S(2)}) async-start(), calls=%async_computation.25 | async-start | bytes 245760
  446.5 216.2 %reduce-scatter.40.cloned.1.call-start = ((), (), s32[]{:S(2)}) async-start(), calls=%async_computation.21 | async-start | bytes 368640 | tf_op jit(solution)/shard_map/reduce_scatter | solution.py:369
  447.8 238.8 %reduce-scatter.50.cloned.1.call-start = ((), (), s32[]{:S(2)}) async-start(), calls=%async_computation.26 | async-start | bytes 491520
  450.6 259.8 %reduce-scatter.54.cloned.1.call-start = ((), (), s32[]{:S(2)}) async-start(), calls=%async_computation.28 | async-start | bytes 491520
  453.6 280.1 %reduce-scatter.56.cloned.1.call-start = ((), (), s32[]{:S(2)}) async-start(), calls=%async_computation.29 | async-start | bytes 491520
  456.6 305.5 %reduce-scatter.44.cloned.1.call-start = ((), (), s32[]{:S(2)}) async-start(), calls=%async_computation.23 | async-start | bytes 1474560 | tf_op jit(solution)/shard_map/reduce_scatter | solution.py:387
  459.9 330.6 %reduce-scatter.42.cloned.1.call-start = ((), (), s32[]{:S(2)}) async-start(), calls=%async_computation.22 | async-start | bytes 1474560 | tf_op jit(solution)/shard_map/reduce_scatter | solution.py:381
  (175 other events, 2773.2 us)
Sparse Core Ops, SparseCore 0:
  14.9 37.5 all-reduce.12
  58.1 34.5 all-reduce.14
  103.8 35.5 all-reduce.16
  148.7 36.7 all-reduce.28
  209.8 37.6 all-reduce.26
  264.4 34.9 all-reduce.18
  310.1 34.5 all-reduce.20
  361.0 33.6 all-reduce.22
  404.3 36.7 all-reduce.24
  443.5 19.1 reduce-scatter.65
  465.3 19.3 reduce-scatter.51
  487.0 19.3 reduce-scatter.57
  509.0 19.7 reduce-scatter.59
  531.2 19.7 reduce-scatter.61
  553.4 19.7 reduce-scatter.63
  575.6 19.7 reduce-scatter.67
  597.8 19.7 reduce-scatter.45
  620.1 19.7 reduce-scatter.47
  642.5 20.2 reduce-scatter.39
  665.7 20.8 reduce-scatter.49
  689.6 20.7 reduce-scatter.53
  712.9 20.7 reduce-scatter.55
  736.4 25.7 reduce-scatter.43
  764.7 25.7 reduce-scatter.41
where the time goes:
time: 801 us; the launch traced here: 799 us
  waiting for transfers between devices  624 us (78%)
  other arithmetic  62.2 us (8%)
  matrix products  54.6 us (7%)
  local copies, waits for them, and re-layouts  30 us (4%)
  between operations  16.8 us (2%)
  starting transfers between devices  11.1 us (1%)
    unnamed x36, waiting for transfers between devices  228 us
    psum x3, waiting for transfers between devices, attention_back(): lax.psum(partial_grad.astype(jnp.bfloat16), 'tensor').astype(jnp.float32)  98.1 us
    psum x2, waiting for transfers between devices, layer_forward(): lax.psum(jnp.dot(mixed, w_attn, preferred_element_type=jnp.float32).astyp...  73.1 us
    psum x2, waiting for transfers between devices, layer_forward(): lax.psum(jnp.dot(active, w_outer, preferred_element_type=jnp.float32).ast...  71.5 us
    psum x2, waiting for transfers between devices, feed_forward_back(): lax.psum(jnp.einsum('sf,df->sd', hidden_low, w_inner, preferred_element_t...  68.8 us
    unnamed x373, local copies, waits for them, and re-layouts  28.4 us
    reduce_scatter x1, waiting for transfers between devices, local(): lax.psum_scatter(every_part[11].astype(jnp.bfloat16), 'dp', scatter_dimen...  26.5 us
    reduce_scatter x1, waiting for transfers between devices, local(): lax.psum_scatter(every_part[13].astype(jnp.bfloat16), 'dp', scatter_dimen...  26.4 us
  transfers between devices with their start and end apart: 28, of which 27 were waited for; matrix products, arithmetic and copies ran while one was open for 8% of the time, Pallas kernels for 0%

commit v1 on v0

v1 whole, which is shorter than its diff:
```python
import functools

import jax
import jax.numpy as jnp
from jax import lax
from jax.experimental import pallas as pl
from jax.experimental.pallas import tpu as pltpu
from jax.sharding import PartitionSpec as P

HEAD_DIM = 64
EPS = 1e-05
MESH = pl.DeviceIdType.MESH
F32 = jnp.float32
BF16 = jnp.bfloat16


def mm(a, b):
    return lax.dot_general(a, b, (((1,), (0,)), ((), ())), preferred_element_type=F32)


def mm_nt(a, b):
    return lax.dot_general(a, b, (((1,), (1,)), ((), ())), preferred_element_type=F32)


def mm_tn(a, b):
    return lax.dot_general(a, b, (((0,), (0,)), ((), ())), preferred_element_type=F32)


def standard(v):
    center = v - jnp.mean(v, axis=-1, keepdims=True)
    rate = lax.rsqrt(jnp.mean(center * center, axis=-1, keepdims=True) + EPS)
    return center * rate, rate


def norm_back(grad, n, rate, gain):
    e = grad * gain
    return rate * (
        e - jnp.mean(e, axis=-1, keepdims=True) - n * jnp.mean(e * n, axis=-1, keepdims=True)
    )


def column_sum(v):
    return jnp.sum(v, axis=0, keepdims=True)


def kernel(dims, *refs):
    C, S, D, G, F, NT, ND, fused = dims
    R = S // NT
    H = G // HEAD_DIM
    scale = HEAD_DIM**-0.5
    (
        frames, cot, gain1, shift1, w_q, q_b, w_k, w_v, v_b, w_a, a_b,
        gain2, shift2, w_i, i_b, w_o, o_b,
    ) = refs[:17]
    lo_out, lg_out, gi_out, go_out, gx_out, ga_out, sm_out = refs[17:24]
    (
        xbuf, dybuf, wqkv, abuf, qkv, pbuf, obuf, hbuf, cbuf, gpbuf, zbuf,
        part, got, ybuf, dubuf, dhbuf, ghbuf, dqkv, dxbuf,
        gi, go, gx, ga, ri, ro, rx, ra, sm, smr, smd, smdr,
        rs_s, rs_r, ag_s, ag_r, sc_s, sc_r, dp_s, dp_r, se_s, se_r,
    ) = refs[24:]

    sec = lax.axis_index("section")
    me = lax.axis_index("tensor")
    dp = lax.axis_index("dp")

    def peer(o):
        return lax.rem(me + o, NT)

    def dpeer(o):
        return lax.rem(dp + o, ND)

    def clip(c):
        return pl.ds(pl.multiple_of(c * S, S), S)

    def rows(c, t):
        return pl.ds(pl.multiple_of(c * S + t * R, R), R)

    def scatter(ph, c, o):
        return pltpu.make_async_remote_copy(
            src_ref=part.at[ph, rows(c, peer(o))],
            dst_ref=got.at[ph, c, o - 1],
            send_sem=rs_s.at[ph, c, o - 1],
            recv_sem=rs_r.at[ph, c, o - 1],
            device_id={"tensor": peer(o)},
            device_id_type=MESH,
        )

    gathered = (cbuf, ghbuf, ybuf, dxbuf)

    def gather(ph, c, o):
        return pltpu.make_async_remote_copy(
            src_ref=gathered[ph].at[rows(c, me)],
            dst_ref=gathered[ph].at[rows(c, me)],
            send_sem=ag_s.at[ph, c, o - 1],
            recv_sem=ag_r.at[ph, c, o - 1],
            device_id={"tensor": peer(o)},
            device_id_type=MESH,
        )

    def across(ph, c, o):
        src, dst = ((ybuf, xbuf), (dxbuf, dybuf))[ph]
        return pltpu.make_async_remote_copy(
            src_ref=src.at[rows(c, me)],
            dst_ref=dst.at[rows(c, me)],
            send_sem=sc_s.at[ph, c, o],
            recv_sem=sc_r.at[ph, c, o],
            device_id={"section": 1 - sec, "tensor": peer(o)},
            device_id_type=MESH,
        )

    terms = ((gi, ri), (go, ro), (gx, rx), (ga, ra))

    def spread(k, o):
        src, dst = terms[k]
        n = dst.shape[1]
        return pltpu.make_async_remote_copy(
            src_ref=src.at[pl.ds(pl.multiple_of(dpeer(o) * n, n), n)],
            dst_ref=dst.at[o - 1],
            send_sem=dp_s.at[k, o - 1],
            recv_sem=dp_r.at[k, o - 1],
            device_id={"dp": dpeer(o)},
            device_id_type=MESH,
        )

    def small_tensor(o):
        return pltpu.make_async_remote_copy(
            src_ref=sm,
            dst_ref=smr.at[o - 1],
            send_sem=se_s.at[o - 1],
            recv_sem=se_r.at[o - 1],
            device_id={"tensor": peer(o)},
            device_id_type=MESH,
        )

    def small_dp(o):
        return pltpu.make_async_remote_copy(
            src_ref=smd,
            dst_ref=smdr.at[o - 1],
            send_sem=dp_s.at[4, o - 1],
            recv_sem=dp_r.at[4, o - 1],
            device_id={"dp": dpeer(o)},
            device_id_type=MESH,
        )

    def start_all(make, *at):
        for o in range(1, NT):
            make(*at, o).start()

    def land(make, *at):
        for o in range(1, NT):
            make(*at, o).wait_recv()

    def summed(ph, c):
        land(scatter, ph, c)
        total = part[ph, rows(c, me), :].astype(F32)
        for o in range(1, NT):
            total = total + got[ph, c, o - 1].astype(F32)
        return total

    def each(body):
        def step(c, carry):
            body(c)
            return carry

        lax.fori_loop(0, C, step, 0)

    barrier = pltpu.get_barrier_semaphore()
    for o in range(1, NT):
        pl.semaphore_signal(barrier, 1, device_id={"tensor": peer(o)}, device_id_type=MESH)
    for o in range(NT):
        pl.semaphore_signal(
            barrier, 1, device_id={"section": 1 - sec, "tensor": peer(o)}, device_id_type=MESH
        )
    greeted = 2 * NT - 1
    if fused:
        for o in range(1, ND):
            pl.semaphore_signal(barrier, 1, device_id={"dp": dpeer(o)}, device_id_type=MESH)
        greeted += ND - 1

    wqkv[:, 0:G] = w_q[...]
    wqkv[:, G : 2 * G] = w_k[...]
    wqkv[:, 2 * G : 3 * G] = w_v[...]
    sm[...] = jnp.zeros_like(sm)
    smd[...] = jnp.zeros_like(smd)

    @pl.when(sec == 0)
    def _():
        xbuf[...] = frames[...]

    @pl.when(sec == 1)
    def _():
        dybuf[...] = cot[...]

    pl.semaphore_wait(barrier, greeted)

    def attention(c):
        @pl.when(sec == 1)
        def _():
            for o in range(NT):
                across(0, c, o).wait_recv()

        n, _ = standard(xbuf[clip(c), :].astype(F32))
        a = (n * gain1[...] + shift1[...]).astype(BF16)
        abuf[clip(c), :] = a
        pre = mm(a, wqkv[...])
        qkv[clip(c), 0:G] = (pre[:, 0:G] + q_b[...]).astype(BF16)
        qkv[clip(c), G : 2 * G] = pre[:, G : 2 * G].astype(BF16)
        qkv[clip(c), 2 * G : 3 * G] = (pre[:, 2 * G :] + v_b[...]).astype(BF16)
        for h in range(H):
            at = [slice(i * G + h * HEAD_DIM, i * G + (h + 1) * HEAD_DIM) for i in range(3)]
            q, k, v = [qkv[clip(c), s] for s in at]
            s = mm_nt(q, k) * scale
            p = jnp.exp(s - jnp.max(s, axis=-1, keepdims=True))
            p = p / jnp.sum(p, axis=-1, keepdims=True)
            pbuf[c, h] = p
            obuf[clip(c), at[0]] = mm(p.astype(BF16), v).astype(BF16)
        part[0, clip(c), :] = mm(obuf[clip(c), :], w_a[...]).astype(BF16)
        start_all(scatter, 0, c)

    each(attention)

    def middle(c):
        h = xbuf[rows(c, me), :].astype(F32) + summed(0, c) + a_b[...]
        hbuf[c] = h
        n, _ = standard(h)
        cbuf[rows(c, me), :] = (n * gain2[...] + shift2[...]).astype(BF16)
        start_all(gather, 0, c)

    each(middle)

    def feed(c):
        land(gather, 0, c)
        u = mm(cbuf[clip(c), :], w_i[...]) + i_b[...]
        cumulative = 0.5 * (1.0 + lax.erf(u * (0.5**0.5)))
        z = (u * cumulative).astype(BF16)
        zbuf[clip(c), :] = z
        part[1, clip(c), :] = mm(z, w_o[...]).astype(BF16)
        start_all(scatter, 1, c)
        gpbuf[clip(c), :] = cumulative + u * (jnp.exp(-0.5 * u * u) * 0.3989422804014327)

    each(feed)

    def finish(c):
        y = hbuf[c] + summed(1, c) + o_b[...]
        ybuf[rows(c, me), :] = y.astype(BF16)

        @pl.when(sec == 0)
        def _():
            for o in range(NT):
                across(0, c, o).start()

        start_all(gather, 2, c)

    each(finish)

    def feed_back(c):
        @pl.when(sec == 0)
        def _():
            for o in range(NT):
                across(1, c, o).wait_recv()

        gy = dybuf[clip(c), :]
        smd[8:9, :] += column_sum(gy.astype(F32))
        du = mm_nt(gy, w_o[...]) * gpbuf[clip(c), :]
        smd[9:10, 0:F] += column_sum(du)
        du = du.astype(BF16)
        dubuf[clip(c), :] = du
        part[2, clip(c), :] = mm_nt(du, w_i[...]).astype(BF16)
        start_all(scatter, 2, c)

    each(feed_back)

    def weight_grad(out, left, right):
        n = left.shape[1]
        for low in range(0, n, 256):
            high = min(low + 256, n)
            out[low:high, :] = mm_tn(left[:, low:high], right[...]).astype(BF16)

    def send_terms(k):
        if fused:
            for o in range(1, ND):
                spread(k, o).start()

    weight_grad(gi, cbuf, dubuf)
    send_terms(0)
    weight_grad(go, zbuf, dybuf)
    send_terms(1)

    def middle_back(c):
        dc = summed(2, c)
        n, rate = standard(hbuf[c])
        sm[2:3, :] += column_sum(dc * n)
        sm[3:4, :] += column_sum(dc)
        dh = dybuf[rows(c, me), :].astype(F32) + norm_back(dc, n, rate, gain2[...])
        sm[4:5, :] += column_sum(dh)
        dhbuf[c] = dh
        ghbuf[rows(c, me), :] = dh.astype(BF16)
        start_all(gather, 1, c)

    each(middle_back)

    def attention_back(c):
        land(gather, 1, c)
        do = mm_nt(ghbuf[clip(c), :], w_a[...]).astype(BF16)
        for h in range(H):
            at = [slice(i * G + h * HEAD_DIM, i * G + (h + 1) * HEAD_DIM) for i in range(3)]
            q, k, v = [qkv[clip(c), s] for s in at]
            do_h = do[:, at[0]]
            p = pbuf[c, h]
            dv = mm_tn(p.astype(BF16), do_h)
            dp_h = mm_nt(do_h, v)
            ds = (p * (dp_h - jnp.sum(p * dp_h, axis=-1, keepdims=True))).astype(BF16)
            dq = mm(ds, k) * scale
            dk = mm_tn(ds, q) * scale
            smd[10:11, at[0]] += column_sum(dq)
            smd[11:12, at[0]] += column_sum(dv)
            for s, grad in zip(at, (dq, dk, dv)):
                dqkv[clip(c), s] = grad.astype(BF16)
        part[3, clip(c), :] = mm_nt(dqkv[clip(c), :], wqkv[...]).astype(BF16)
        start_all(scatter, 3, c)

    each(attention_back)
    weight_grad(gx, abuf, dqkv)
    send_terms(2)
    weight_grad(ga, obuf, ghbuf)
    send_terms(3)

    def input_back(c):
        da = summed(3, c)
        n, rate = standard(xbuf[rows(c, me), :].astype(F32))
        sm[0:1, :] += column_sum(da * n)
        sm[1:2, :] += column_sum(da)
        dx = dhbuf[c] + norm_back(da, n, rate, gain1[...])
        dxbuf[rows(c, me), :] = dx.astype(BF16)

        @pl.when(sec == 1)
        def _():
            for o in range(NT):
                across(1, c, o).start()

        start_all(gather, 3, c)

    each(input_back)

    start_all(small_tensor)
    land(small_tensor)
    total = sm[...]
    for o in range(1, NT):
        total = total + smr[o - 1]
    smd[0:8, :] = total
    if fused:
        for o in range(1, ND):
            small_dp(o).start()

    each(lambda c: land(gather, 2, c))
    lo_out[...] = ybuf[...]
    each(lambda c: land(gather, 3, c))
    lg_out[...] = dxbuf[...]

    if fused:
        for k, out in enumerate((gi_out, go_out, gx_out, ga_out)):
            src, dst = terms[k]
            n = dst.shape[1]
            total = src[pl.ds(pl.multiple_of(dp * n, n), n), :].astype(F32)
            for o in range(1, ND):
                spread(k, o).wait_recv()
                total = total + dst[o - 1].astype(F32)
            out[...] = total
        total = smd[...]
        for o in range(1, ND):
            small_dp(o).wait_recv()
            total = total + smdr[o - 1]
        sm_out[...] = total
    else:
        gi_out[...] = gi[...]
        go_out[...] = go[...]
        gx_out[...] = gx[...]
        ga_out[...] = ga[...]
        sm_out[...] = smd[...]

    def sent(c):
        for ph in range(4):
            for o in range(1, NT):
                scatter(ph, c, o).wait_send()
                gather(ph, c, o).wait_send()

        @pl.when(sec == 0)
        def _():
            for o in range(NT):
                across(0, c, o).wait_send()

        @pl.when(sec == 1)
        def _():
            for o in range(NT):
                across(1, c, o).wait_send()

    each(sent)
    for o in range(1, NT):
        small_tensor(o).wait_send()
    if fused:
        for o in range(1, ND):
            small_dp(o).wait_send()
            for k in range(4):
                spread(k, o).wait_send()


def local(NT, ND, *args):
    C, S, D = args[0].shape
    G = args[4].shape[2]
    F = args[13].shape[2]
    T = C * S
    R = S // NT
    H = G // HEAD_DIM
    fused = (D // ND) % 16 == 0 and (G // ND) % 16 == 0 and (F // ND) % 16 == 0
    dims = (C, S, D, G, F, NT, ND, fused)
    operands = [v.reshape(T, D) for v in args[:2]]
    operands += [v[0] if v.ndim == 3 else v for v in args[2:]]
    M = ND if fused else 1
    term = F32 if fused else BF16
    shapes = [
        jax.ShapeDtypeStruct((T, D), BF16),
        jax.ShapeDtypeStruct((T, D), BF16),
        jax.ShapeDtypeStruct((D // M, F), term),
        jax.ShapeDtypeStruct((F // M, D), term),
        jax.ShapeDtypeStruct((D // M, 3 * G), term),
        jax.ShapeDtypeStruct((G // M, D), term),
        jax.ShapeDtypeStruct((16, D), F32),
    ]
    peers = max(M - 1, 1)

    def slots(*shape):
        return pltpu.VMEM((peers,) + shape, BF16) if fused else pltpu.VMEM((1, 16, 128), BF16)

    dma = pltpu.SemaphoreType.DMA
    scratch = [
        pltpu.VMEM((T, D), BF16),
        pltpu.VMEM((T, D), BF16),
        pltpu.VMEM((D, 3 * G), BF16),
        pltpu.VMEM((T, D), BF16),
        pltpu.VMEM((T, 3 * G), BF16),
        pltpu.VMEM((C, H, S, S), F32),
        pltpu.VMEM((T, G), BF16),
        pltpu.VMEM((C, R, D), F32),
        pltpu.VMEM((T, D), BF16),
        pltpu.VMEM((T, F), F32),
        pltpu.VMEM((T, F), BF16),
        pltpu.VMEM((4, T, D), BF16),
        pltpu.VMEM((4, C, NT - 1, R, D), BF16),
        pltpu.VMEM((T, D), BF16),
        pltpu.VMEM((T, F), BF16),
        pltpu.VMEM((C, R, D), F32),
        pltpu.VMEM((T, D), BF16),
        pltpu.VMEM((T, 3 * G), BF16),
        pltpu.VMEM((T, D), BF16),
        pltpu.VMEM((D, F), BF16),
        pltpu.VMEM((F, D), BF16),
        pltpu.VMEM((D, 3 * G), BF16),
        pltpu.VMEM((G, D), BF16),
        slots(D // M, F),
        slots(F // M, D),
        slots(D // M, 3 * G),
        slots(G // M, D),
        pltpu.VMEM((8, D), F32),
        pltpu.VMEM((NT - 1, 8, D), F32),
        pltpu.VMEM((16, D), F32),
        pltpu.VMEM((peers, 16, D), F32),
        dma((4, C, NT - 1)),
        dma((4, C, NT - 1)),
        dma((4, C, NT - 1)),
        dma((4, C, NT - 1)),
        dma((2, C, NT)),
        dma((2, C, NT)),
        dma((5, peers)),
        dma((5, peers)),
        dma((NT - 1,)),
        dma((NT - 1,)),
    ]
    spec = pl.BlockSpec(memory_space=pltpu.VMEM)
    lo, lg, gi, go, gx, ga, sm = pl.pallas_call(
        functools.partial(kernel, dims),
        out_shape=shapes,
        in_specs=[spec] * 17,
        out_specs=[spec] * 7,
        scratch_shapes=scratch,
        compiler_params=pltpu.CompilerParams(
            collective_id=0, has_side_effects=True, vmem_limit_bytes=56 * 1024 * 1024
        ),
        cost_estimate=pl.CostEstimate(
            flops=6 * T * D * (4 * G + 2 * F), bytes_accessed=8 * D * F, transcendentals=T * F
        ),
        name="layers",
    )(*operands)
    if not fused:
        gi, go, gx, ga = [
            lax.psum_scatter(v, "dp", scatter_dimension=0, tiled=True).astype(F32)
            for v in (gi, go, gx, ga)
        ]
        sm = lax.psum(sm, "dp")
    at = lax.axis_index("dp")

    def small(row, width):
        n = width // ND
        return lax.dynamic_slice(sm, (row, at * n), (1, n))

    return (
        lo.reshape(1, C, S, D),
        lg.reshape(1, C, S, D),
        small(0, D),
        small(1, D),
        gx[None, :, 0:G],
        small(10, G),
        gx[None, :, G : 2 * G],
        gx[None, :, 2 * G :],
        small(11, G),
        ga[None],
        small(4, D),
        small(2, D),
        small(3, D),
        gi[None],
        small(9, F),
        go[None],
        small(8, D),
    )


def solution(mesh):
    cols = P("section", None, "tensor")
    rows = P("section", "tensor", None)
    wide = P("section", None)
    part = P("section", "tensor")
    clips = P("dp", None, None)
    in_specs = (
        clips, clips, wide, wide, cols, part, cols, cols, part, rows, wide,
        wide, wide, cols, part, rows, wide,
    )
    acts = P("section", "dp", None, None)
    vec = P("section", "dp")
    col_grad = P("section", "dp", "tensor")
    both = P("section", ("tensor", "dp"))
    row_grad = P("section", ("tensor", "dp"), None)
    out_specs = (
        acts, acts, vec, vec, col_grad, both, col_grad, col_grad, both, row_grad, vec,
        vec, vec, col_grad, both, row_grad, vec,
    )
    return jax.shard_map(
        functools.partial(local, mesh.shape["tensor"], mesh.shape["dp"]),
        mesh=mesh,
        in_specs=in_specs,
        out_specs=out_specs,
        check_vma=False,
    )
```

time: 801 us -> 185 us (0.23)
  waiting for transfers between devices: 624 us -> 0 us
  Pallas kernels: 0 us -> 169 us
  other arithmetic: 62.2 us -> 0 us
  matrix products: 54.6 us -> 0 us
  local copies, waits for them, and re-layouts: 30 us -> 13.5 us
  between operations: 16.8 us -> 0.7 us
  starting transfers between devices: 11.1 us -> 0 us
    psum x9 -> x0, waiting for transfers between devices: 311 us -> none  [the longest x3 98.1 us: attention_back(): lax.psum(partial_grad.astype(jnp.bfloat16), 'tensor').astype(jnp.float32)]
    unnamed x36 -> x0, waiting for transfers between devices: 228 us -> none
    pallas_call x0 -> x1, Pallas kernels: none -> 169 us  [local(): pl.pallas_call(functools.partial(kernel, dims), out_shape=shapes, in_spec...]
    reduce_scatter x3 -> x0, waiting for transfers between devices: 74.4 us -> none  [the longest x1 26.5 us: local(): lax.psum_scatter(every_part[11].astype(jnp.bfloat16), 'dp', scatter_dimen...]
    dot_general x63 -> x0, matrix products: 54.6 us -> none  [the longest x3 6.58 us: layer_forward(): jnp.dot(normed_two, w_inner, preferred_element_type=jnp.float32)]
    reduce_sum x35 -> x0, other arithmetic: 39.1 us -> none  [the longest x11 13 us: normalize(): spread = jnp.mean(center * center, axis=-1, keepdims=True)]
    unnamed x373 -> x20, local copies, waits for them, and re-layouts: 28.4 us -> 8.53 us
    convert_element_type x31 -> x0, other arithmetic: 13.6 us -> none  [the longest x12 10.3 us: local(): reduced = (lax.psum_scatter(every_part[0].astype(jnp.bfloat16), 'dp', sca...]
  transfers between devices with their start and end apart: 28 -> 0, of which waited for: 27 -> 0; matrix products, arithmetic and copies ran while one was open for 8% -> 0% of each run, Pallas kernels for 0% -> 0%
where the time goes in v1:
time: 185 us; the launch traced here: 183 us
  Pallas kernels  169 us (91%)
  local copies, waits for them, and re-layouts  13.5 us (7%)
    pallas_call x1, Pallas kernels, local(): pl.pallas_call(functools.partial(kernel, dims), out_shape=shapes, in_spec...  169 us
    unnamed x20, local copies, waits for them, and re-layouts  8.53 us

profile of v1, /device:TPU:0, one launch (start us, length us, event | category | flops | bytes accessed | tf_op | source)
XLA Modules:
  0.0 183.1 jit_solution(7725799495923582553)
XLA Ops:
  0.7 0.0 copy-start.4
  0.7 1.9 %copy.34 = bf16[1,768,192]{2,1,0:T(8,128)(2,1)} copy(bf16[1,768,192]{1,2,0:T(8,128)(2,1)} %param.21) | data formatting | bytes 589824 | tf_op args[4]
  2.6 1.9 %copy.35 = bf16[1,768,192]{2,1,0:T(8,128)(2,1)} copy(bf16[1,768,192]{1,2,0:T(8,128)(2,1)} %param.23) | data formatting | bytes 589824 | tf_op args[6]
  4.5 0.0 copy-done.4
  4.5 0.9 copy.36
  5.4 168.9 %layers.1 = (bf16[256,768]{1,0:T(8,128)(2,1)}, bf16[256,768]{1,0:T(8,128)(2,1)}, f32[192,768]{1,0:T(8,128)}, f32[192,768]{1,0:T(8,128)}, f32[192,576]{1,0:T(8,12...) custom-call(bf16[256,768]{1,0:T(8,128)(2,1)} %bitcast.29, bf16[256,768]{1,0:T(8,128)(2,1)} %bitcast.30, f32[1,768]{1,0:T(1,128)} %refs_2_.1, ...), custom_call_target="tpu_custom_call" | custom-call | flops 2717908992 | bytes 4718592 | tf_op jit(solution)/shard_map/layers/pallas_call | solution.py:480
  174.3 0.0 copy-start.3
  174.3 0.0 copy-start.2
  174.3 1.6 constant_dynamic-slice_fusion
  175.9 0.0 copy-start.5
  175.9 2.0 %slice_bitcast_fusion = (f32[1,192,192]{2,1,0:T(8,128)}, f32[1,192,192]{2,1,0:T(8,128)}, f32[1,192,192]{2,1,0:T(8,128)}) fusion(f32[192,576]{1,0:T(8,128)} %get-tuple-element.27), kind=kLoop, calls=%fused_computation | loop fusion | bytes 884736 | tf_op jit(solution)/shard_map/broadcast_in_dim | solution.py:514
  177.9 0.0 copy-start.1
  177.9 1.4 constant_dynamic-slice_fusion.5
  179.3 0.0 copy-done.3
  179.3 0.7 copy.42
  180.0 0.0 copy-done.2
  180.0 0.0 copy-start
  180.0 0.7 copy.43
  180.8 0.0 copy-done.5
  180.8 0.7 copy.44
  181.4 0.0 copy-done.1
  181.4 0.8 copy.45
  182.3 0.0 copy-done
  182.3 0.8 copy.46
Async XLA Ops:
  0.7 3.8 %copy-start.4 = (bf16[1,768,192]{1,2,0:T(8,128)(2,1)S(1)}, bf16[1,768,192]{1,2,0:T(8,128)(2,1)}, u32[]{:S(2)}) copy-start(bf16[1,768,192]{1,2,0:T(8,128)(2,1)} %param.24) | copy-start | bytes 884740
  174.3 5.0 %copy-start.3 = (bf16[256,768]{1,0:T(8,128)(2,1)S(1)}, bf16[256,768]{1,0:T(8,128)(2,1)}, u32[]{:S(2)}) copy-start(bf16[256,768]{1,0:T(8,128)(2,1)} %get-tuple-element.24) | copy-start | bytes 1179652
  174.3 5.7 %copy-start.2 = (bf16[256,768]{1,0:T(8,128)(2,1)S(1)}, bf16[256,768]{1,0:T(8,128)(2,1)}, u32[]{:S(2)}) copy-start(bf16[256,768]{1,0:T(8,128)(2,1)} %get-tuple-element.25) | copy-start | bytes 1179652
  175.9 4.9 %copy-start.5 = (f32[48,768]{1,0:T(8,128)S(1)}, f32[48,768]{1,0:T(8,128)}, u32[]{:S(2)}) copy-start(f32[48,768]{1,0:T(8,128)} %get-tuple-element.28) | copy-start | bytes 442372
  177.9 3.5 %copy-start.1 = (f32[192,768]{1,0:T(8,128)S(1)}, f32[192,768]{1,0:T(8,128)}, u32[]{:S(2)}) copy-start(f32[192,768]{1,0:T(8,128)} %get-tuple-element.29) | copy-start | bytes 1769476
  180.0 2.2 %copy-start = (f32[192,768]{1,0:T(8,128)S(1)}, f32[192,768]{1,0:T(8,128)}, u32[]{:S(2)}) copy-start(f32[192,768]{1,0:T(8,128)} %get-tuple-element.30) | copy-start | bytes 1769476

commit v2 on v1

--- a/solution.py
+++ b/solution.py
@@ -55,9 +55,9 @@
     lo_out, lg_out, gi_out, go_out, gx_out, ga_out, sm_out = refs[17:24]
     (
         xbuf, dybuf, wqkv, abuf, qkv, pbuf, obuf, hbuf, cbuf, gpbuf, zbuf,
-        part, got, ybuf, dubuf, dhbuf, ghbuf, dqkv, dxbuf,
+        part, got, ybuf, dzbuf, dubuf, dhbuf, ghbuf, dqkv, dxbuf,
         gi, go, gx, ga, ri, ro, rx, ra, sm, smr, smd, smdr,
-        rs_s, rs_r, ag_s, ag_r, sc_s, sc_r, dp_s, dp_r, se_s, se_r,
+        wfull, ofull, hfull, wa_s, wa_r, oa_s, oa_r, rs_s, rs_r, ag_s, ag_r, sc_s, sc_r, dp_s, dp_r, se_s, se_r,
     ) = refs[24:]
 
     sec = lax.axis_index("section")
@@ -109,6 +109,26 @@
             device_id_type=MESH,
         )
 
+    def weight_copy(o):
+        return pltpu.make_async_remote_copy(
+            src_ref=wfull.at[me],
+            dst_ref=wfull.at[me],
+            send_sem=wa_s.at[o - 1],
+            recv_sem=wa_r.at[o - 1],
+            device_id={"tensor": peer(o)},
+            device_id_type=MESH,
+        )
+
+    def heads_copy(c, o):
+        return pltpu.make_async_remote_copy(
+            src_ref=ofull.at[me, clip(c)],
+            dst_ref=ofull.at[me, clip(c)],
+            send_sem=oa_s.at[c, o - 1],
+            recv_sem=oa_r.at[c, o - 1],
+            device_id={"tensor": peer(o)},
+            device_id_type=MESH,
+        )
+
     terms = ((gi, ri), (go, ro), (gx, rx), (ga, ra))
 
     def spread(k, o):
@@ -146,6 +166,10 @@
     def start_all(make, *at):
         for o in range(1, NT):
             make(*at, o).start()
+
+    def gone(make, *at):
+        for o in range(NT):
+            make(*at, o).wait_send()
 
     def land(make, *at):
         for o in range(1, NT):
@@ -178,9 +202,9 @@
             pl.semaphore_signal(barrier, 1, device_id={"dp": dpeer(o)}, device_id_type=MESH)
         greeted += ND - 1
 
-    wqkv[:, 0:G] = w_q[...]
-    wqkv[:, G : 2 * G] = w_k[...]
-    wqkv[:, 2 * G : 3 * G] = w_v[...]
+    wqkv[0:G, :] = w_q[...]
+    wqkv[G : 2 * G, :] = w_k[...]
+    wqkv[2 * G : 3 * G, :] = w_v[...]
     sm[...] = jnp.zeros_like(sm)
     smd[...] = jnp.zeros_like(smd)
 
@@ -188,11 +212,23 @@
     def _():
         xbuf[...] = frames[...]
 
+    def outer_back(c):
+        gy = dybuf[clip(c), :]
+        smd[8:9, :] += column_sum(gy.astype(F32))
+        dzbuf[clip(c), :] = mm_nt(gy, w_o[...])
+
     @pl.when(sec == 1)
     def _():
         dybuf[...] = cot[...]
+        each(outer_back)
 
     pl.semaphore_wait(barrier, greeted)
+
+    @pl.when(sec == 1)
+    def _():
+        wfull[me] = w_a[...]
+        start_all(weight_copy)
+        land(weight_copy)
 
     def attention(c):
         @pl.when(sec == 1)
@@ -203,7 +239,7 @@
         n, _ = standard(xbuf[clip(c), :].astype(F32))
         a = (n * gain1[...] + shift1[...]).astype(BF16)
         abuf[clip(c), :] = a
-        pre = mm(a, wqkv[...])
+        pre = mm_nt(a, wqkv[...])
         qkv[clip(c), 0:G] = (pre[:, 0:G] + q_b[...]).astype(BF16)
         qkv[clip(c), G : 2 * G] = pre[:, G : 2 * G].astype(BF16)
         qkv[clip(c), 2 * G : 3 * G] = (pre[:, 2 * G :] + v_b[...]).astype(BF16)
@@ -215,8 +251,16 @@
             p = p / jnp.sum(p, axis=-1, keepdims=True)
             pbuf[c, h] = p
             obuf[clip(c), at[0]] = mm(p.astype(BF16), v).astype(BF16)
-        part[0, clip(c), :] = mm(obuf[clip(c), :], w_a[...]).astype(BF16)
-        start_all(scatter, 0, c)
+
+        @pl.when(sec == 0)
+        def _():
+            part[0, clip(c), :] = mm(obuf[clip(c), :], w_a[...]).astype(BF16)
+            start_all(scatter, 0, c)
+
+        @pl.when(sec == 1)
+        def _():
+            ofull[me, clip(c), :] = obuf[clip(c), :]
+            start_all(heads_copy, c)
 
     each(attention)
 
@@ -227,16 +271,42 @@
         cbuf[rows(c, me), :] = (n * gain2[...] + shift2[...]).astype(BF16)
         start_all(gather, 0, c)
 
-    each(middle)
+    def middle_whole(c):
+        land(heads_copy, c)
+        h = xbuf[clip(c), :].astype(F32) + a_b[...]
+        for t in range(NT):
+            h = h + mm(ofull[t, clip(c), :], wfull[t])
+        hfull[...] = h
+        hbuf[c] = hfull[pl.ds(pl.multiple_of(me * R, R), R), :]
+        n, _ = standard(h)
+        cbuf[clip(c), :] = (n * gain2[...] + shift2[...]).astype(BF16)
+
+    @pl.when(sec == 0)
+    def _():
+        each(middle)
+
+    @pl.when(sec == 1)
+    def _():
+        each(middle_whole)
+
+    def feed_out(c):
+        part[1, clip(c), :] = mm(zbuf[clip(c), :], w_o[...]).astype(BF16)
+        start_all(scatter, 1, c)
 
     def feed(c):
-        land(gather, 0, c)
+        @pl.when(sec == 0)
+        def _():
+            land(gather, 0, c)
+
         u = mm(cbuf[clip(c), :], w_i[...]) + i_b[...]
         cumulative = 0.5 * (1.0 + lax.erf(u * (0.5**0.5)))
         z = (u * cumulative).astype(BF16)
         zbuf[clip(c), :] = z
-        part[1, clip(c), :] = mm(z, w_o[...]).astype(BF16)
-        start_all(scatter, 1, c)
+
+        @pl.when(sec == 0)
+        def _():
+            feed_out(c)
+
         gpbuf[clip(c), :] = cumulative + u * (jnp.exp(-0.5 * u * u) * 0.3989422804014327)
 
     each(feed)
@@ -250,19 +320,20 @@
             for o in range(NT):
                 across(0, c, o).start()
 
-        start_all(gather, 2, c)
-
-    each(finish)
+    @pl.when(sec == 0)
+    def _():
+        each(finish)
+        each(lambda c: gone(across, 0, c))
+        each(lambda c: start_all(gather, 2, c))
 
     def feed_back(c):
         @pl.when(sec == 0)
         def _():
             for o in range(NT):
                 across(1, c, o).wait_recv()
-
-        gy = dybuf[clip(c), :]
-        smd[8:9, :] += column_sum(gy.astype(F32))
-        du = mm_nt(gy, w_o[...]) * gpbuf[clip(c), :]
+            outer_back(c)
+
+        du = dzbuf[clip(c), :] * gpbuf[clip(c), :]
         smd[9:10, 0:F] += column_sum(du)
         du = du.astype(BF16)
         dubuf[clip(c), :] = du
@@ -282,10 +353,21 @@
             for o in range(1, ND):
                 spread(k, o).start()
 
-    weight_grad(gi, cbuf, dubuf)
-    send_terms(0)
-    weight_grad(go, zbuf, dybuf)
-    send_terms(1)
+    def feed_weights():
+        weight_grad(gi, cbuf, dubuf)
+        send_terms(0)
+        weight_grad(go, zbuf, dybuf)
+        send_terms(1)
+
+    def attention_weights():
+        weight_grad(gx, abuf, dqkv)
+        send_terms(2)
+        weight_grad(ga, obuf, ghbuf)
+        send_terms(3)
+
+    @pl.when(sec == 0)
+    def _():
+        feed_weights()
 
     def middle_back(c):
         dc = summed(2, c)
@@ -317,14 +399,14 @@
             smd[11:12, at[0]] += column_sum(dv)
             for s, grad in zip(at, (dq, dk, dv)):
                 dqkv[clip(c), s] = grad.astype(BF16)
-        part[3, clip(c), :] = mm_nt(dqkv[clip(c), :], wqkv[...]).astype(BF16)
+        part[3, clip(c), :] = mm(dqkv[clip(c), :], wqkv[...]).astype(BF16)
         start_all(scatter, 3, c)
 
     each(attention_back)
-    weight_grad(gx, abuf, dqkv)
-    send_terms(2)
-    weight_grad(ga, obuf, ghbuf)
-    send_terms(3)
+
+    @pl.when(sec == 0)
+    def _():
+        attention_weights()
 
     def input_back(c):
         da = summed(3, c)
@@ -339,9 +421,18 @@
             for o in range(NT):
                 across(1, c, o).start()
 
-        start_all(gather, 3, c)
-
     each(input_back)
+
+    @pl.when(sec == 1)
+    def _():
+        each(lambda c: gone(across, 1, c))
+        each(feed_out)
+        feed_weights()
+        attention_weights()
+        each(finish)
+        each(lambda c: start_all(gather, 2, c))
+
+    each(lambda c: start_all(gather, 3, c))
 
     start_all(small_tensor)
     land(small_tensor)
@@ -380,22 +471,29 @@
         sm_out[...] = smd[...]
 
     def sent(c):
-        for ph in range(4):
+        for ph in range(1, 4):
             for o in range(1, NT):
                 scatter(ph, c, o).wait_send()
                 gather(ph, c, o).wait_send()
 
         @pl.when(sec == 0)
         def _():
-            for o in range(NT):
-                across(0, c, o).wait_send()
+            for o in range(1, NT):
+                scatter(0, c, o).wait_send()
+                gather(0, c, o).wait_send()
 
         @pl.when(sec == 1)
         def _():
-            for o in range(NT):
-                across(1, c, o).wait_send()
+            for o in range(1, NT):
+                heads_copy(c, o).wait_send()
 
     each(sent)
+
+    @pl.when(sec == 1)
+    def _():
+        for o in range(1, NT):
+            weight_copy(o).wait_send()
+
     for o in range(1, NT):
         small_tensor(o).wait_send()
     if fused:
@@ -416,6 +514,8 @@
     dims = (C, S, D, G, F, NT, ND, fused)
     operands = [v.reshape(T, D) for v in args[:2]]
     operands += [v[0] if v.ndim == 3 else v for v in args[2:]]
+    for at in (4, 6, 7):
+        operands[at] = operands[at].T
     M = ND if fused else 1
     term = F32 if fused else BF16
     shapes = [
@@ -436,7 +536,7 @@
     scratch = [
         pltpu.VMEM((T, D), BF16),
         pltpu.VMEM((T, D), BF16),
-        pltpu.VMEM((D, 3 * G), BF16),
+        pltpu.VMEM((3 * G, D), BF16),
         pltpu.VMEM((T, D), BF16),
         pltpu.VMEM((T, 3 * G), BF16),
         pltpu.VMEM((C, H, S, S), F32),
@@ -448,6 +548,7 @@
         pltpu.VMEM((4, T, D), BF16),
         pltpu.VMEM((4, C, NT - 1, R, D), BF16),
         pltpu.VMEM((T, D), BF16),
+        pltpu.VMEM((T, F), F32),
         pltpu.VMEM((T, F), BF16),
         pltpu.VMEM((C, R, D), F32),
         pltpu.VMEM((T, D), BF16),
@@ -465,6 +566,13 @@
         pltpu.VMEM((NT - 1, 8, D), F32),
         pltpu.VMEM((16, D), F32),
         pltpu.VMEM((peers, 16, D), F32),
+        pltpu.VMEM((NT, G, D), BF16),
+        pltpu.VMEM((NT, T, G), BF16),
+        pltpu.VMEM((S, D), F32),
+        dma((NT - 1,)),
+        dma((NT - 1,)),
+        dma((C, NT - 1)),
+        dma((C, NT - 1)),
         dma((4, C, NT - 1)),
         dma((4, C, NT - 1)),
         dma((4, C, NT - 1)),

time: 185 us -> 150 us (0.81)
  Pallas kernels: 169 us -> 140 us
  local copies, waits for them, and re-layouts: 13.5 us -> 8.74 us
    pallas_call x1, Pallas kernels: 169 us -> 140 us  [local(): pl.pallas_call(functools.partial(kernel, dims), out_shape=shapes, in_spec...]
    unnamed x20 -> x15, local copies, waits for them, and re-layouts: 8.53 us -> 3.8 us
where the time goes in v2:
time: 150 us; the launch traced here: 149 us
  Pallas kernels  140 us (93%)
  local copies, waits for them, and re-layouts  8.74 us (6%)
    pallas_call x1, Pallas kernels, local(): pl.pallas_call(functools.partial(kernel, dims), out_shape=shapes, in_spec...  140 us
    unnamed x15, local copies, waits for them, and re-layouts  3.8 us

profile of v2, /device:TPU:0, one launch (start us, length us, event | category | flops | bytes accessed | tf_op | source)
XLA Modules:
  0.0 149.0 jit_solution(3599586449286432705)
XLA Ops:
  0.7 139.5 %layers.1 = (bf16[256,768]{1,0:T(8,128)(2,1)}, bf16[256,768]{1,0:T(8,128)(2,1)}, f32[192,768]{1,0:T(8,128)}, f32[192,768]{1,0:T(8,128)}, f32[192,576]{1,0:T(8,12...) custom-call(bf16[256,768]{1,0:T(8,128)(2,1)} %bitcast.32, bf16[256,768]{1,0:T(8,128)(2,1)} %bitcast.33, f32[1,768]{1,0:T(1,128)} %refs_2_.1, ...), custom_call_target="tpu_custom_call" | custom-call | flops 2717908992 | bytes 4718592 | tf_op jit(solution)/shard_map/layers/pallas_call | solution.py:588
  140.2 0.0 copy-start.3
  140.2 0.0 copy-start.2
  140.2 1.4 constant_dynamic-slice_fusion.5
  141.6 1.6 %constant_dynamic-slice_fusion = (f32[1,192]{1,0:T(1,128)}, f32[1,192]{1,0:T(1,128)}, f32[1,192]{1,0:T(1,128)}, f32[1,192]{1,0:T(1,128)}, f32[1,192]{1,0:T(1,128)}, /*index=5*/f32[1,192]{1,0:T(1,128)}, f32[1,192]{1,0:T(1,128)}) fusion(f32[16,768]{1,0:T(8,128)} %get-tuple-element.26, s32[]{:T(128)S(6)} %select_n.4), kind=kLoop, calls=%fused_computation.3 | loop fusion | bytes 10756 | tf_op jit(solution)/shard_map/dynamic_slice | solution.py:612
  143.2 0.0 copy-start.4
  143.2 2.0 %slice_bitcast_fusion = (f32[1,192,192]{2,1,0:T(8,128)}, f32[1,192,192]{2,1,0:T(8,128)}, f32[1,192,192]{2,1,0:T(8,128)}) fusion(f32[192,576]{1,0:T(8,128)} %get-tuple-element.27), kind=kLoop, calls=%fused_computation | loop fusion | bytes 884736 | tf_op jit(solution)/shard_map/broadcast_in_dim | solution.py:622
  145.2 0.0 copy-start.1
  145.2 0.0 copy-done.3
  145.2 0.7 copy.39
  145.9 0.0 copy-done.2
  145.9 0.0 copy-start
  145.9 0.7 copy.40
  146.7 0.0 copy-done.4
  146.7 0.7 copy.41
  147.3 0.0 copy-done.1
  147.3 0.8 copy.42
  148.1 0.0 copy-done
  148.2 0.8 copy.43
Async XLA Ops:
  140.2 5.0 %copy-start.3 = (bf16[256,768]{1,0:T(8,128)(2,1)S(1)}, bf16[256,768]{1,0:T(8,128)(2,1)}, u32[]{:S(2)}) copy-start(bf16[256,768]{1,0:T(8,128)(2,1)} %get-tuple-element.24) | copy-start | bytes 1179652
  140.2 5.7 %copy-start.2 = (bf16[256,768]{1,0:T(8,128)(2,1)S(1)}, bf16[256,768]{1,0:T(8,128)(2,1)}, u32[]{:S(2)}) copy-start(bf16[256,768]{1,0:T(8,128)(2,1)} %get-tuple-element.25) | copy-start | bytes 1179652
  143.2 3.5 %copy-start.4 = (f32[48,768]{1,0:T(8,128)S(1)}, f32[48,768]{1,0:T(8,128)}, u32[]{:S(2)}) copy-start(f32[48,768]{1,0:T(8,128)} %get-tuple-element.28) | copy-start | bytes 442372
  145.2 2.2 %copy-start.1 = (f32[192,768]{1,0:T(8,128)S(1)}, f32[192,768]{1,0:T(8,128)}, u32[]{:S(2)}) copy-start(f32[192,768]{1,0:T(8,128)} %get-tuple-element.29) | copy-start | bytes 1769476
  145.9 2.2 %copy-start = (f32[192,768]{1,0:T(8,128)S(1)}, f32[192,768]{1,0:T(8,128)}, u32[]{:S(2)}) copy-start(f32[192,768]{1,0:T(8,128)} %get-tuple-element.30) | copy-start | bytes 1769476
